TPU v7x, 256 devices: a whole 4x4x8 slice. The times are simulated.
256 devices in a mesh: sx: 4 (over x_lo, core), sy: 2 (over x_hi), fsdp: 32 (over z, y).
Axes of the slice: x: 4 (x_hi: 2, x_lo: 2; x = x_hi * 2 + x_lo), y: 4, z: 8, core: 2. Of those that a mesh axis runs over, the one named last changes fastest.
Arguments:
- x_code: bfloat16 [32, 32, 32, 1536], P('fsdp', 'sx', 'sy'), may hold values from -6 to 6
- x_exp: int32 [32, 32, 32, 12], P('fsdp', 'sx', 'sy'), may hold values from -2 to 2
- dw_kernel: float32 [7, 7, 1536], replicated, may hold values from -1.2 to 1.2
- dw_bias: float32 [1536], replicated, may hold values from -4 to 4
- ln_gain: float32 [1536], replicated, may hold values from 0.1 to 1.9
- ln_bias: float32 [1536], replicated, may hold values from -3 to 3
- w_up: bfloat16 [1536, 3072], P('fsdp'), may hold values from -0.15625 to 0.15625
- b_up: float32 [3072], replicated, may hold values from -3 to 3
- w_down: bfloat16 [3072, 1536], P(None, 'fsdp'), may hold values from -0.109375 to 0.109375
- b_down: float32 [1536], replicated, may hold values from -3 to 3
- layer_scale: float32 [1536], replicated, may hold values from 0.3 to 1.5
- cotangent: bfloat16 [32, 32, 32, 1536], P('fsdp', 'sx', 'sy'), may hold values from -6 to 6
Outputs:
- block_out: bfloat16 [32, 32, 32, 1536], P('fsdp', 'sx', 'sy')
- grad_input: bfloat16 [32, 32, 32, 1536], P('fsdp', 'sx', 'sy')
- grad_kernel: float32 [7, 7, 1536], replicated
- grad_gain: float32 [1536], replicated
- grad_scale: float32 [1536], replicated
All inputs are finite; a program needn't handle non-finite values.
Results may differ from a plain program's by a relative error of at most 0.006.
Values may be sent and summed in bfloat16 or wider, within the bound.
A program may use at most 192 MiB of HBM per device.

v0:
```python
import jax
import jax.numpy as jnp
from jax import lax
from jax.sharding import PartitionSpec as P

CG = 128
KW = 7


def with_halo(shard, sides, width):
    for axis, dim in sides:
        devices, length = (lax.axis_size(axis), shard.shape[dim])
        up = [(i, (i + 1) % devices) for i in range(devices - 1)]
        down = [(j, i) for i, j in up]
        last = lax.slice_in_dim(shard, length - width, length, axis=dim)
        initial = lax.slice_in_dim(shard, 0, width, axis=dim)
        before = lax.ppermute(last, axis, up)
        after = lax.ppermute(initial, axis, down)
        shard = jnp.concatenate([before, shard, after], axis=dim)
    return shard


def gelu_tanh(v):
    return jax.nn.gelu(v, approximate=True)


def on_device(
    x_code,
    x_exp,
    dw_kernel,
    dw_bias,
    ln_gain,
    ln_bias,
    w_up,
    b_up,
    w_down,
    b_down,
    layer_scale,
    cotangent,
):
    code = x_code[0]
    rows, cols, chans = code.shape
    factor = jnp.exp2(x_exp[0].astype(jnp.float32))
    grouped = code.astype(jnp.float32).reshape(rows, cols, chans // CG, CG) * factor[..., None]
    scaled = grouped.reshape(rows, cols, chans).astype(jnp.bfloat16)
    up_full, down_full = (
        lax.all_gather(w_up, "fsdp", axis=0, tiled=True),
        lax.all_gather(w_down, "fsdp", axis=1, tiled=True),
    )
    padded_x = with_halo(scaled[None], (("sx", 1), ("sy", 2)), 3)[0].astype(jnp.float32)
    conv = jnp.zeros((rows, cols, chans), jnp.float32) + dw_bias
    for i in range(KW):
        for j in range(KW):
            conv = conv + dw_kernel[i, j] * padded_x[i : i + rows, j : j + cols]
    mean_val = jnp.mean(conv, axis=-1, keepdims=True)
    centred = conv - mean_val
    rstd = lax.rsqrt(jnp.mean(centred * centred, axis=-1, keepdims=True) + 1e-06)
    normed = centred * rstd
    ln_out = (normed * ln_gain + ln_bias).astype(jnp.bfloat16).reshape(rows * cols, chans)
    pre = jnp.dot(ln_out, up_full, preferred_element_type=jnp.float32) + b_up
    act, gelu_back = jax.vjp(gelu_tanh, pre)
    mlp = jnp.dot(act.astype(jnp.bfloat16), down_full, preferred_element_type=jnp.float32) + b_down
    mlp = mlp.reshape(rows, cols, chans)
    block_out = (scaled.astype(jnp.float32) + layer_scale * mlp).astype(jnp.bfloat16)
    grad_f = cotangent[0].astype(jnp.float32)
    scale_term = jnp.sum(grad_f * mlp, axis=(0, 1))
    d_mlp = (layer_scale * grad_f).astype(jnp.bfloat16).reshape(rows * cols, chans)
    d_act = lax.dot_general(
        d_mlp, down_full, (((1,), (1,)), ((), ())), preferred_element_type=jnp.float32
    )
    d_pre = gelu_back(d_act)[0].astype(jnp.bfloat16)
    d_ln = lax.dot_general(
        d_pre, up_full, (((1,), (1,)), ((), ())), preferred_element_type=jnp.float32
    )
    d_ln = d_ln.reshape(rows, cols, chans)
    gain_term = jnp.sum(d_ln * normed, axis=(0, 1))
    d_norm = d_ln * ln_gain
    d_conv = rstd * (
        d_norm
        - jnp.mean(d_norm, axis=-1, keepdims=True)
        - normed * jnp.mean(d_norm * normed, axis=-1, keepdims=True)
    )
    kernel_rows = []
    for i in range(KW):
        kernel_cols = []
        for j in range(KW):
            kernel_cols.append(jnp.sum(d_conv * padded_x[i : i + rows, j : j + cols], axis=(0, 1)))
        kernel_rows.append(jnp.stack(kernel_cols))
    kernel_term = jnp.stack(kernel_rows)
    padded_grad = with_halo(d_conv[None].astype(jnp.bfloat16), (("sx", 1), ("sy", 2)), 3).astype(
        jnp.float32
    )[0]
    back_conv = grad_f
    for i in range(KW):
        for j in range(KW):
            back_conv = (
                back_conv
                + dw_kernel[i, j] * padded_grad[6 - i : 6 - i + rows, 6 - j : 6 - j + cols]
            )
    grad_input = back_conv.astype(jnp.bfloat16)
    grad_kernel, grad_gain, grad_scale = lax.psum(
        (kernel_term, gain_term, scale_term), ("sx", "sy", "fsdp")
    )
    return (block_out[None], grad_input[None], grad_kernel, grad_gain, grad_scale)


def solution(mesh):
    placed = (
        P("fsdp", "sx", "sy", None),
        P("fsdp", "sx", "sy", None),
        P(),
        P(),
        P(),
        P(),
        P("fsdp", None),
        P(),
        P(None, "fsdp"),
        P(),
        P(),
        P("fsdp", "sx", "sy", None),
    )
    return jax.shard_map(
        on_device,
        mesh=mesh,
        in_specs=placed,
        out_specs=(P("fsdp", "sx", "sy", None), P("fsdp", "sx", "sy", None), P(), P(), P()),
        check_vma=False,
    )
```

profile of v0, /device:TPU:1, one launch (start us, length us, event | category | flops | bytes accessed | tf_op | source)
XLA Modules:
  0.0 522.2 jit_solution(14191568544540321584)
XLA Ops:
  7.2 0.7 all-gather.3.cloned.1.call-update
  7.9 0.7 all-gather.5.cloned.1.call-update
  8.7 0.9 exponential_bitcast_fusion
  9.6 0.1 copy.18
  9.7 0.3 mul.1066
  10.0 0.1 mul.1067
  10.3 4.5 collective-permute-start
  14.8 1.9 collective-permute-start.1
  16.8 0.3 slice_reduce_fusion.48
  17.2 0.9 slice_reduce_fusion.47
  18.3 3.0 collective-permute-done.1
  21.3 0.1 pad_maximum_fusion.3
  21.4 4.4 collective-permute-start.2
  25.8 1.3 collective-permute-start.3
  27.1 0.8 slice_reduce_fusion.46
  27.8 0.2 collective-permute-done.2
  28.1 5.4 %collective-permute-done.3 = bf16[1,14,3,1536]{3,2,1,0:T(4,128)(2,1)S(1)} collective-permute-done((bf16[1,14,3,1536]{3,2,1,0:T(4,128)(2,1)S(1)}, bf16[1,14,3,1536]{3,2,1,0:T(4,128)(2,1)S(1)}, u32[]{:S(2)}, u32[]{:S(2)}) %collective-permute-start.3) | collective-permute-done | bytes 129056 | tf_op jit(solution)/shard_map/ppermute | solution.py:18
  33.5 0.4 fusion.7
  34.2 9.4 %fusion.84 = (f32[8,16]{1,0:T(8,128)S(1)}, f32[8,16,1536]{2,1,0:T(8,128)S(1)}) fusion(f32[14,22,1536]{2,1,0:T(8,128)S(1)} %fusion.7, f32[1536]{0:T(1024)} %get-tuple-element.103, f32[1536]{0:T(1024)} %get-tuple-element.104, f32[1536]{0:T(1024)S(1)} %get-tuple-element.57, f32[1536]{0:T(1024)S(1)} %get-tuple-element.58, f32[1536]{0:T(1024)S(1)} %get-tuple-element.59, ...), kind=kLoop, calls=%fused_computation.267 | loop fusion | flops 19464064 | bytes 39629312 | tf_op jit(solution)/shard_map/reduce_sum | solution.py:55
  43.7 0.2 multiply_reduce_fusion.52
  43.9 1.7 add_convert_fusion.1
  45.6 71.9 %all-gather.3.cloned.1.call-done = bf16[1536,3072]{1,0:T(8,128)(2,1)} async-done(((bf16[48,3072]{1,0:T(8,128)(2,1)}), bf16[1536,3072]{1,0:T(8,128)(2,1)}) %all-gather.3.cloned.1.call-update) | async-done | bytes 9437200 | tf_op jit(solution)/shard_map/all_gather | solution.py:47
  117.5 6.4 %convolution_add_fusion = f32[128,3072]{1,0:T(8,128)} fusion(bf16[128,1536]{1,0:T(8,128)(2,1)} %bitcast.55, bf16[1536,3072]{1,0:T(8,128)(2,1)} %all-gather.3.cloned.1.call-done, f32[3072]{0:T(1024)S(1)} %copy-done.50), kind=kOutput, calls=%fused_computation | convolution fusion | flops 1208352768 | bytes 11415552 | tf_op jit(solution)/shard_map/dot_general | solution.py:60
  124.0 96.8 %all-gather.5.cloned.1.call-done = bf16[3072,1536]{0,1:T(8,128)(2,1)} async-done(((bf16[3072,48]{0,1:T(8,128)(2,1)}), bf16[3072,1536]{0,1:T(8,128)(2,1)}) %all-gather.5.cloned.1.call-update) | async-done | bytes 9437200 | tf_op jit(solution)/shard_map/all_gather | solution.py:48
  220.8 8.9 %fusion.61 = (f32[1536]{0:T(1024)}, bf16[128,1536]{1,0:T(8,128)(2,1)}, f32[128,1536]{1,0:T(8,128)}) fusion(bf16[1,8,16,1536]{3,2,1,0:T(8,128)(2,1)} %param.23, f32[1536]{0:T(1024)S(1)} %copy-done.51, f32[1536]{0:T(1024)S(1)} %copy-done.54, bf16[3072,1536]{0,1:T(8,128)(2,1)} %all-gather.5.cloned.1.call-done, f32[128,3072]{1,0:T(8,128)} %convolution_add_fusion), kind=kOutput, calls=%fused_computation.119 | convolution fusion | flops 1212676608 | bytes 12601344 | tf_op jit(solution)/shard_map/dot_general | solution.py:62
  229.7 13.3 %multiply_reduce_fusion.51 = (f32[128]{0:T(128)S(1)}, f32[128,1536]{1,0:T(8,128)}) fusion(f32[1536]{0:T(1024)S(1)} %copy-done.8, bf16[1536,3072]{1,0:T(8,128)(2,1)} %all-gather.3.cloned.1.call-done, f32[128,3072]{1,0:T(8,128)} %convolution_add_fusion, bf16[128,1536]{1,0:T(8,128)(2,1)} %get-tuple-element.118, ...), kind=kOutput, calls=%fused_computation.172 | convolution fusion | flops 2424176640 | bytes 21633536 | tf_op jit(solution)/shard_map/dot_general | solution.py:72
  243.0 0.1 div.17
  243.1 2.4 multiply_reduce_fusion
  245.5 2.6 multiply_reduce_fusion.1
  248.1 1.4 multiply_reduce_fusion.37
  249.6 2.0 multiply_reduce_fusion.19
  251.6 0.9 add_convert_fusion
  253.1 4.1 collective-permute-start.4
  257.2 1.9 collective-permute-start.5
  259.2 0.1 stack.217
  259.3 0.1 stack.226
  259.8 3.9 collective-permute-done.5
  263.7 0.1 fusion.83
  263.8 0.1 fusion.85
  263.9 4.3 collective-permute-start.6
  268.3 1.3 collective-permute-start.7
  269.6 0.7 copy-done.2
  270.4 75.8 %all-reduce = (f32[1536]{0:T(1024)}, f32[1536]{0:T(1024)}) all-reduce(f32[1536]{0:T(1024)S(1)} %copy-done.49, f32[1536]{0:T(1024)S(1)} %copy-done.53), channel_id=1, replica_groups=mesh['sx'=4,'sy'=2,'fsdp'=32] {'sx','sy','fsdp'}, use_global_device_ids=true, to_apply=%region_55.0 | all-reduce | flops 3072 | bytes 24576 | tf_op jit(solution)/shard_map/psum | solution.py:101
  346.3 0.6 copy-done.6
  347.0 1.4 maximum_convert_fusion
  348.4 7.7 %fusion.72 = bf16[1,8,16,1536]{3,2,1,0:T(8,128)(2,1)} fusion(f32[14,22,1536]{2,1,0:T(8,128)S(1)} %maximum_convert_fusion, f32[1536]{0:T(1024)} %get-tuple-element.103, f32[1536]{0:T(1024)} %get-tuple-element.104, f32[1536]{0:T(1024)S(1)} %get-tuple-element.57, f32[1536]{0:T(1024)S(1)} %copy-done.10, f32[1536]{0:T(1024)S(1)} %copy-done.12, ...), kind=kLoop, calls=%fused_computation.191 | loop fusion | flops 19660800 | bytes 39622656 | tf_op jit(solution)/shard_map/broadcast_in_dim | solution.py:104
  356.1 157.8 %all-reduce.3.cloned.1.call-done = f32[7,7,1536]{2,1,0:T(8,128)} async-done(((f32[7,7,1536]{2,1,0:T(8,128)}), f32[7,7,1536]{2,1,0:T(8,128)}) %all-reduce.3.cloned.1.call-update) | async-done | bytes 301072 | tf_op jit(solution)/shard_map/psum | solution.py:101
  514.0 1.7 copy.26
  (184 shorter events, 1.3 us)
Async XLA Ops:
  7.2 110.4 %all-gather.3.cloned.1.call-start = ((), (), s32[]{:S(2)}) async-start(), calls=%async_computation | async-start | bytes 9732096 | tf_op jit(solution)/shard_map/all_gather | solution.py:47
  7.9 212.9 %all-gather.5.cloned.1.call-start = ((), (), s32[]{:S(2)}) async-start(), calls=%async_computation.1 | async-start | bytes 9732096 | tf_op jit(solution)/shard_map/all_gather | solution.py:48
  8.7 505.3 %all-reduce.3.cloned.1.call-start = ((), (), s32[]{:S(2)}) async-start(), calls=%async_computation.2 | async-start | bytes 688128 | tf_op jit(solution)/shard_map/psum | solution.py:101
  10.3 8.0 %collective-permute-start = (bf16[1,3,16,1536]{3,2,1,0:T(8,128)(2,1)S(1)}, bf16[1,3,16,1536]{3,2,1,0:T(8,128)(2,1)S(1)}, u32[]{:S(2)}, u32[]{:S(2)}) collective-permute-start(bf16[1,3,16,1536]{3,2,1,0:T(8,128)(2,1)S(1)} %get-tuple-element.121), channel_id=1, source_target_pairs={{0,64},{64,128},{128,192},{1,65},{65,129},{129,193},{2,66},{66,130... | collective-permute-start | bytes 442376 | tf_op jit(solution)/shard_map/ppermute | solution.py:17
  14.8 6.5 %collective-permute-start.1 = (bf16[1,3,16,1536]{3,2,1,0:T(8,128)(2,1)S(1)}, bf16[1,3,16,1536]{3,2,1,0:T(8,128)(2,1)S(1)}, u32[]{:S(2)}, u32[]{:S(2)}) collective-permute-start(bf16[1,3,16,1536]{3,2,1,0:T(8,128)(2,1)S(1)} %get-tuple-element.122), channel_id=1, source_target_pairs={{64,0},{128,64},{192,128},{65,1},{129,65},{193,129},{66,2},{130,66... | collective-permute-start | bytes 442376 | tf_op jit(solution)/shard_map/ppermute | solution.py:18
  17.1 16.8 %copy-start.9 = (f32[1536]{0:T(1024)}, f32[1536]{0:T(1024)S(1)}, u32[]{:S(2)}) copy-start(f32[1536]{0:T(1024)S(1)} %get-tuple-element.58) | copy-start | bytes 18436
  17.1 16.8 %copy-start.11 = (f32[1536]{0:T(1024)}, f32[1536]{0:T(1024)S(1)}, u32[]{:S(2)}) copy-start(f32[1536]{0:T(1024)S(1)} %get-tuple-element.59) | copy-start | bytes 18436
  17.1 16.8 %copy-start.13 = (f32[1536]{0:T(1024)}, f32[1536]{0:T(1024)S(1)}, u32[]{:S(2)}) copy-start(f32[1536]{0:T(1024)S(1)} %get-tuple-element.60) | copy-start | bytes 18436
  17.1 16.8 %copy-start.15 = (f32[1536]{0:T(1024)}, f32[1536]{0:T(1024)S(1)}, u32[]{:S(2)}) copy-start(f32[1536]{0:T(1024)S(1)} %get-tuple-element.61) | copy-start | bytes 18436
  17.1 16.8 %copy-start.17 = (f32[1536]{0:T(1024)}, f32[1536]{0:T(1024)S(1)}, u32[]{:S(2)}) copy-start(f32[1536]{0:T(1024)S(1)} %get-tuple-element.62) | copy-start | bytes 18436
  17.1 16.8 %copy-start.19 = (f32[1536]{0:T(1024)}, f32[1536]{0:T(1024)S(1)}, u32[]{:S(2)}) copy-start(f32[1536]{0:T(1024)S(1)} %get-tuple-element.63) | copy-start | bytes 18436
  17.1 16.8 %copy-start.21 = (f32[1536]{0:T(1024)}, f32[1536]{0:T(1024)S(1)}, u32[]{:S(2)}) copy-start(f32[1536]{0:T(1024)S(1)} %get-tuple-element.64) | copy-start | bytes 18436
  17.1 16.8 %copy-start.22 = (f32[1536]{0:T(1024)}, f32[1536]{0:T(1024)S(1)}, u32[]{:S(2)}) copy-start(f32[1536]{0:T(1024)S(1)} %get-tuple-element.65) | copy-start | bytes 18436
  17.2 16.8 %copy-start.23 = (f32[1536]{0:T(1024)}, f32[1536]{0:T(1024)S(1)}, u32[]{:S(2)}) copy-start(f32[1536]{0:T(1024)S(1)} %get-tuple-element.66) | copy-start | bytes 18436
  17.2 16.8 %copy-start.24 = (f32[1536]{0:T(1024)}, f32[1536]{0:T(1024)S(1)}, u32[]{:S(2)}) copy-start(f32[1536]{0:T(1024)S(1)} %get-tuple-element.67) | copy-start | bytes 18436
  17.2 16.8 %copy-start.25 = (f32[1536]{0:T(1024)}, f32[1536]{0:T(1024)S(1)}, u32[]{:S(2)}) copy-start(f32[1536]{0:T(1024)S(1)} %get-tuple-element.68) | copy-start | bytes 18436
  17.2 16.8 %copy-start.26 = (f32[1536]{0:T(1024)}, f32[1536]{0:T(1024)S(1)}, u32[]{:S(2)}) copy-start(f32[1536]{0:T(1024)S(1)} %get-tuple-element.69) | copy-start | bytes 18436
  17.2 16.8 %copy-start.27 = (f32[1536]{0:T(1024)}, f32[1536]{0:T(1024)S(1)}, u32[]{:S(2)}) copy-start(f32[1536]{0:T(1024)S(1)} %get-tuple-element.70) | copy-start | bytes 18436
  17.2 16.8 %copy-start.28 = (f32[1536]{0:T(1024)}, f32[1536]{0:T(1024)S(1)}, u32[]{:S(2)}) copy-start(f32[1536]{0:T(1024)S(1)} %get-tuple-element.71) | copy-start | bytes 18436
  17.2 16.8 %copy-start.29 = (f32[1536]{0:T(1024)}, f32[1536]{0:T(1024)S(1)}, u32[]{:S(2)}) copy-start(f32[1536]{0:T(1024)S(1)} %get-tuple-element.72) | copy-start | bytes 18436
  17.2 16.8 %copy-start.30 = (f32[1536]{0:T(1024)}, f32[1536]{0:T(1024)S(1)}, u32[]{:S(2)}) copy-start(f32[1536]{0:T(1024)S(1)} %get-tuple-element.73) | copy-start | bytes 18436
  17.2 16.8 %copy-start.31 = (f32[1536]{0:T(1024)}, f32[1536]{0:T(1024)S(1)}, u32[]{:S(2)}) copy-start(f32[1536]{0:T(1024)S(1)} %get-tuple-element.74) | copy-start | bytes 18436
  18.2 15.9 %copy-start.37 = (f32[1536]{0:T(1024)}, f32[1536]{0:T(1024)S(1)}, u32[]{:S(2)}) copy-start(f32[1536]{0:T(1024)S(1)} %get-tuple-element.80) | copy-start | bytes 18436
  18.2 15.9 %copy-start.38 = (f32[1536]{0:T(1024)}, f32[1536]{0:T(1024)S(1)}, u32[]{:S(2)}) copy-start(f32[1536]{0:T(1024)S(1)} %get-tuple-element.81) | copy-start | bytes 18436
  18.2 15.9 %copy-start.39 = (f32[1536]{0:T(1024)}, f32[1536]{0:T(1024)S(1)}, u32[]{:S(2)}) copy-start(f32[1536]{0:T(1024)S(1)} %get-tuple-element.82) | copy-start | bytes 18436
  18.2 15.9 %copy-start.40 = (f32[1536]{0:T(1024)}, f32[1536]{0:T(1024)S(1)}, u32[]{:S(2)}) copy-start(f32[1536]{0:T(1024)S(1)} %get-tuple-element.83) | copy-start | bytes 18436
  18.2 15.9 %copy-start.41 = (f32[1536]{0:T(1024)}, f32[1536]{0:T(1024)S(1)}, u32[]{:S(2)}) copy-start(f32[1536]{0:T(1024)S(1)} %get-tuple-element.84) | copy-start | bytes 18436
  18.2 15.9 %copy-start.42 = (f32[1536]{0:T(1024)}, f32[1536]{0:T(1024)S(1)}, u32[]{:S(2)}) copy-start(f32[1536]{0:T(1024)S(1)} %get-tuple-element.85) | copy-start | bytes 18436
  18.2 15.9 %copy-start.43 = (f32[1536]{0:T(1024)}, f32[1536]{0:T(1024)S(1)}, u32[]{:S(2)}) copy-start(f32[1536]{0:T(1024)S(1)} %get-tuple-element.86) | copy-start | bytes 18436
  18.2 15.9 %copy-start.44 = (f32[1536]{0:T(1024)}, f32[1536]{0:T(1024)S(1)}, u32[]{:S(2)}) copy-start(f32[1536]{0:T(1024)S(1)} %get-tuple-element.87) | copy-start | bytes 18436
  18.3 15.9 %copy-start.45 = (f32[1536]{0:T(1024)}, f32[1536]{0:T(1024)S(1)}, u32[]{:S(2)}) copy-start(f32[1536]{0:T(1024)S(1)} %get-tuple-element.88) | copy-start | bytes 18436
  18.3 15.9 %copy-start.46 = (f32[1536]{0:T(1024)}, f32[1536]{0:T(1024)S(1)}, u32[]{:S(2)}) copy-start(f32[1536]{0:T(1024)S(1)} %get-tuple-element.89) | copy-start | bytes 18436
  21.4 6.7 %collective-permute-start.2 = (bf16[1,14,3,1536]{3,2,1,0:T(4,128)(2,1)S(1)}, bf16[1,14,3,1536]{3,2,1,0:T(4,128)(2,1)S(1)}, u32[]{:S(2)}, u32[]{:S(2)}) collective-permute-start(bf16[1,14,3,1536]{3,2,1,0:T(4,128)(2,1)S(1)} %get-tuple-element.115), channel_id=1, source_target_pairs={{0,32},{1,33},{2,34},{3,35},{4,36},{5,37},{6,38},{7,39},{8,40},{9,... | collective-permute-start | bytes 387080 | tf_op jit(solution)/shard_map/ppermute | solution.py:17
  25.8 7.7 %collective-permute-start.3 = (bf16[1,14,3,1536]{3,2,1,0:T(4,128)(2,1)S(1)}, bf16[1,14,3,1536]{3,2,1,0:T(4,128)(2,1)S(1)}, u32[]{:S(2)}, u32[]{:S(2)}) collective-permute-start(bf16[1,14,3,1536]{3,2,1,0:T(4,128)(2,1)S(1)} %get-tuple-element.116), channel_id=1, source_target_pairs={{32,0},{33,1},{34,2},{35,3},{36,4},{37,5},{38,6},{39,7},{40,8},{41... | collective-permute-start | bytes 387080 | tf_op jit(solution)/shard_map/ppermute | solution.py:18
  43.7 73.9 %copy-start.50 = (f32[3072]{0:T(1024)S(1)}, f32[3072]{0:T(1024)}, u32[]{:S(2)}) copy-start(f32[3072]{0:T(1024)} %param.19) | copy-start | bytes 36868
  117.5 103.2 %copy-start.51 = (f32[1536]{0:T(1024)S(1)}, f32[1536]{0:T(1024)}, u32[]{:S(2)}) copy-start(f32[1536]{0:T(1024)} %param.22) | copy-start | bytes 18436
  117.5 103.2 %copy-start.54 = (f32[1536]{0:T(1024)S(1)}, f32[1536]{0:T(1024)}, u32[]{:S(2)}) copy-start(f32[1536]{0:T(1024)} %param.21) | copy-start | bytes 18436
  253.1 6.7 %collective-permute-start.4 = (bf16[1,3,16,1536]{3,2,1,0:T(8,128)(2,1)S(1)}, bf16[1,3,16,1536]{3,2,1,0:T(8,128)(2,1)S(1)}, u32[]{:S(2)}, u32[]{:S(2)}) collective-permute-start(bf16[1,3,16,1536]{3,2,1,0:T(8,128)(2,1)S(1)} %get-tuple-element.119), channel_id=1, source_target_pairs={{0,64},{64,128},{128,192},{1,65},{65,129},{129,193},{2,66},{66,130... | collective-permute-start | bytes 442376 | tf_op jit(solution)/shard_map/ppermute | solution.py:17
  257.2 6.5 %collective-permute-start.5 = (bf16[1,3,16,1536]{3,2,1,0:T(8,128)(2,1)S(1)}, bf16[1,3,16,1536]{3,2,1,0:T(8,128)(2,1)S(1)}, u32[]{:S(2)}, u32[]{:S(2)}) collective-permute-start(bf16[1,3,16,1536]{3,2,1,0:T(8,128)(2,1)S(1)} %get-tuple-element.120), channel_id=1, source_target_pairs={{64,0},{128,64},{192,128},{65,1},{129,65},{193,129},{66,2},{130,66... | collective-permute-start | bytes 442376 | tf_op jit(solution)/shard_map/ppermute | solution.py:18
  263.9 82.3 %collective-permute-start.6 = (bf16[1,14,3,1536]{3,2,1,0:T(4,128)(2,1)S(1)}, bf16[1,14,3,1536]{3,2,1,0:T(4,128)(2,1)S(1)}, u32[]{:S(2)}, u32[]{:S(2)}) collective-permute-start(bf16[1,14,3,1536]{3,2,1,0:T(4,128)(2,1)S(1)} %get-tuple-element.111), channel_id=1, source_target_pairs={{0,32},{1,33},{2,34},{3,35},{4,36},{5,37},{6,38},{7,39},{8,40},{9,... | collective-permute-start | bytes 387080 | tf_op jit(solution)/shard_map/ppermute | solution.py:17
  268.3 78.0 %collective-permute-start.7 = (bf16[1,14,3,1536]{3,2,1,0:T(4,128)(2,1)S(1)}, bf16[1,14,3,1536]{3,2,1,0:T(4,128)(2,1)S(1)}, u32[]{:S(2)}, u32[]{:S(2)}) collective-permute-start(bf16[1,14,3,1536]{3,2,1,0:T(4,128)(2,1)S(1)} %get-tuple-element.112), channel_id=1, source_target_pairs={{32,0},{33,1},{34,2},{35,3},{36,4},{37,5},{38,6},{39,7},{40,8},{41... | collective-permute-start | bytes 387080 | tf_op jit(solution)/shard_map/ppermute | solution.py:18
  270.3 78.0 %copy-start.3 = (bf16[1,8,16,1536]{3,2,1,0:T(8,128)(2,1)S(1)}, bf16[1,8,16,1536]{3,2,1,0:T(8,128)(2,1)}, u32[]{:S(2)}) copy-start(bf16[1,8,16,1536]{3,2,1,0:T(8,128)(2,1)} %param.23) | copy-start | bytes 1179652
  270.3 78.0 %copy-start.10 = (f32[1536]{0:T(1024)S(1)}, f32[1536]{0:T(1024)}, u32[]{:S(2)}) copy-start(f32[1536]{0:T(1024)} %copy-done.9) | copy-start | bytes 18436
  270.3 78.0 %copy-start.12 = (f32[1536]{0:T(1024)S(1)}, f32[1536]{0:T(1024)}, u32[]{:S(2)}) copy-start(f32[1536]{0:T(1024)} %copy-done.11) | copy-start | bytes 18436
  270.4 78.0 %copy-start.14 = (f32[1536]{0:T(1024)S(1)}, f32[1536]{0:T(1024)}, u32[]{:S(2)}) copy-start(f32[1536]{0:T(1024)} %copy-done.13) | copy-start | bytes 18436
  270.4 78.0 %copy-start.16 = (f32[1536]{0:T(1024)S(1)}, f32[1536]{0:T(1024)}, u32[]{:S(2)}) copy-start(f32[1536]{0:T(1024)} %copy-done.15) | copy-start | bytes 18436
  270.4 78.0 %copy-start.18 = (f32[1536]{0:T(1024)S(1)}, f32[1536]{0:T(1024)}, u32[]{:S(2)}) copy-start(f32[1536]{0:T(1024)} %copy-done.17) | copy-start | bytes 18436
  270.4 78.0 %copy-start.20 = (f32[1536]{0:T(1024)S(1)}, f32[1536]{0:T(1024)}, u32[]{:S(2)}) copy-start(f32[1536]{0:T(1024)} %copy-done.19) | copy-start | bytes 18436
  (18 other events, 159.1 us)
Sparse Core Ops, SparseCore 0:
  10.6 106.9 all-gather.2
  120.1 100.5 all-gather.4
  270.4 243.4 all-reduce.2
where the time goes:
time: 523 us; the launch traced here: 522 us
  waiting for transfers between devices  340 us (65%)
  blocking collectives  75.8 us (14%)
  other arithmetic  31.2 us (6%)
  matrix products  28.6 us (5%)
  starting transfers between devices  23.8 us (5%)
  between operations  15.1 us (3%)
  local copies, waits for them, and re-layouts  7.13 us (1%)
    psum x1, waiting for transfers between devices, on_device(): lax.psum((kernel_term, gain_term, scale_term), ('sx', 'sy', 'fsdp'))  158 us
    all_gather x1, waiting for transfers between devices, on_device(): lax.all_gather(w_down, 'fsdp', axis=1, tiled=True)  96.8 us
    psum x1, blocking collectives, on_device(): lax.psum((kernel_term, gain_term, scale_term), ('sx', 'sy', 'fsdp'))  75.8 us
    all_gather x1, waiting for transfers between devices, on_device(): lax.all_gather(w_up, 'fsdp', axis=0, tiled=True)  71.9 us
    ppermute x4, starting transfers between devices, with_halo(): before = lax.ppermute(last, axis, up)  17.3 us
    dot_general x1, matrix products, on_device(): lax.dot_general(d_pre, up_full, (((1,), (1,)), ((), ())), preferred_eleme...  13.3 us
    ppermute x4, waiting for transfers between devices, with_halo(): after = lax.ppermute(initial, axis, down)  12.2 us
  transfers between devices with their start and end apart: 11, of which 7 were waited for; matrix products, arithmetic and copies ran while one was open for 6% of the time, Pallas kernels for 0%

commit v1 on v0

--- a/solution.py
+++ b/solution.py
@@ -99,7 +99,7 @@
             )
     grad_input = back_conv.astype(jnp.bfloat16)
     grad_kernel, grad_gain, grad_scale = lax.psum(
-        (kernel_term, gain_term, scale_term), ("sx", "sy", "fsdp")
+        lax.psum((kernel_term, gain_term, scale_term), ("sy", "fsdp")), "sx"
     )
     return (block_out[None], grad_input[None], grad_kernel, grad_gain, grad_scale)
 

time: 523 us -> 972 us (1.86)
  blocking collectives: 75.8 us -> 365 us
  waiting for transfers between devices: 340 us -> 501 us
    psum x1 -> x2, blocking collectives: 75.8 us -> 365 us  [the longest x1 304 us: on_device(): lax.psum((kernel_term, gain_term, scale_term), ('sy', 'fsdp'))]
    psum x1 -> x2, waiting for transfers between devices: 158 us -> 319 us  [the longest x1 251 us: on_device(): lax.psum((kernel_term, gain_term, scale_term), ('sy', 'fsdp'))]
  transfers between devices with their start and end apart: 11 -> 12, of which waited for: 7 -> 8; matrix products, arithmetic and copies ran while one was open for 6% -> 3% of each run, Pallas kernels for 0% -> 0%
where the time goes in v1:
time: 972 us
  waiting for transfers between devices  501 us (52%)
  blocking collectives  365 us (38%)
  other arithmetic  30.7 us (3%)
  matrix products  28.6 us (3%)
  starting transfers between devices  23.9 us (2%)
  between operations  15.7 us (2%)
    psum x1, blocking collectives, on_device(): lax.psum((kernel_term, gain_term, scale_term), ('sy', 'fsdp'))  304 us
    psum x1, waiting for transfers between devices, on_device(): lax.psum((kernel_term, gain_term, scale_term), ('sy', 'fsdp'))  251 us
    all_gather x1, waiting for transfers between devices, on_device(): lax.all_gather(w_down, 'fsdp', axis=1, tiled=True)  96.8 us
    all_gather x1, waiting for transfers between devices, on_device(): lax.all_gather(w_up, 'fsdp', axis=0, tiled=True)  71.9 us
    psum x1, waiting for transfers between devices, on_device(): lax.psum(lax.psum((kernel_term, gain_term, scale_term), ('sy', 'fsdp')),...  67.4 us
    psum x1, blocking collectives, on_device(): lax.psum(lax.psum((kernel_term, gain_term, scale_term), ('sy', 'fsdp')),...  60.7 us
  transfers between devices with their start and end apart: 12, of which 8 were waited for; matrix products, arithmetic and copies ran while one was open for 3% of the time, Pallas kernels for 0%

profile of v1, /device:TPU:1, one launch (start us, length us, event | category | flops | bytes accessed | tf_op | source)
XLA Modules:
  0.0 971.8 jit_solution(17138634087036800721)
XLA Ops:
  7.2 0.7 all-gather.3.cloned.1.call-update
  7.9 0.7 all-gather.5.cloned.1.call-update
  8.7 0.9 exponential_bitcast_fusion
  9.6 0.1 copy.18
  9.7 0.3 mul.1066
  10.0 0.1 mul.1067
  10.3 4.5 collective-permute-start
  14.8 1.9 collective-permute-start.1
  16.8 0.3 slice_reduce_fusion.48
  17.2 0.9 slice_reduce_fusion.47
  18.3 3.0 collective-permute-done.1
  21.3 0.1 pad_maximum_fusion.3
  21.4 4.4 collective-permute-start.2
  25.8 1.3 collective-permute-start.3
  27.1 0.8 slice_reduce_fusion.46
  27.8 0.3 collective-permute-done.2
  28.1 5.4 collective-permute-done.3
  33.5 0.4 fusion.7
  34.2 9.4 fusion.84
  43.7 0.2 multiply_reduce_fusion.52
  43.9 1.7 add_convert_fusion.1
  45.6 71.9 %all-gather.3.cloned.1.call-done = bf16[1536,3072]{1,0:T(8,128)(2,1)} async-done(((bf16[48,3072]{1,0:T(8,128)(2,1)}), bf16[1536,3072]{1,0:T(8,128)(2,1)}) %all-gather.3.cloned.1.call-update) | async-done | bytes 9437200 | tf_op jit(solution)/shard_map/all_gather | solution.py:47
  117.5 6.4 convolution_add_fusion
  124.0 96.8 %all-gather.5.cloned.1.call-done = bf16[3072,1536]{0,1:T(8,128)(2,1)} async-done(((bf16[3072,48]{0,1:T(8,128)(2,1)}), bf16[3072,1536]{0,1:T(8,128)(2,1)}) %all-gather.5.cloned.1.call-update) | async-done | bytes 9437200 | tf_op jit(solution)/shard_map/all_gather | solution.py:48
  220.8 8.9 fusion.61
  229.7 13.3 %multiply_reduce_fusion.51 = (f32[128]{0:T(128)S(1)}, f32[128,1536]{1,0:T(8,128)}) fusion(f32[1536]{0:T(1024)S(1)} %copy-done.8, bf16[1536,3072]{1,0:T(8,128)(2,1)} %all-gather.3.cloned.1.call-done, f32[128,3072]{1,0:T(8,128)} %convolution_add_fusion, bf16[128,1536]{1,0:T(8,128)(2,1)} %get-tuple-element.120, ...), kind=kOutput, calls=%fused_computation.172 | convolution fusion | flops 2424176640 | bytes 21633536 | tf_op jit(solution)/shard_map/dot_general | solution.py:72
  243.0 0.1 div.17
  243.1 2.4 multiply_reduce_fusion
  245.5 2.6 multiply_reduce_fusion.1
  248.1 1.4 multiply_reduce_fusion.37
  249.6 2.0 multiply_reduce_fusion.19
  251.6 0.9 add_convert_fusion
  253.1 4.1 collective-permute-start.4
  257.2 1.9 collective-permute-start.5
  259.8 3.9 collective-permute-done.5
  263.7 0.1 fusion.83
  263.8 0.1 fusion.85
  263.9 4.3 collective-permute-start.6
  268.2 1.3 collective-permute-start.7
  269.6 0.7 copy-done.2
  270.4 303.8 %all-reduce = (f32[1536]{0:T(1024)S(1)}, f32[1536]{0:T(1024)S(1)}) all-reduce(f32[1536]{0:T(1024)S(1)} %copy-done.82, f32[1536]{0:T(1024)S(1)} %copy-done.86), channel_id=1, replica_groups=mesh['sx'=4,'sy'=2,'fsdp'=32] {'sy','fsdp'}, use_global_device_ids=true, to_apply=%region_56.0 | all-reduce | flops 3072 | bytes 24576 | tf_op jit(solution)/shard_map/psum | solution.py:102
  574.2 60.7 %all-reduce.1 = (f32[1536]{0:T(1024)}, f32[1536]{0:T(1024)}) all-reduce(f32[1536]{0:T(1024)S(1)} %get-tuple-element.105, f32[1536]{0:T(1024)S(1)} %get-tuple-element.106), channel_id=1, replica_groups=mesh['sx'=4,'sy'=2,'fsdp'=32] {'sx'}, use_global_device_ids=true, to_apply=%region_57.0 | all-reduce | flops 3072 | bytes 24576 | tf_op jit(solution)/shard_map/psum | solution.py:101
  634.9 0.6 copy-done.6
  636.0 1.5 maximum_convert_fusion
  637.5 251.2 %all-reduce.5.cloned.1.call-done = f32[7,7,1536]{2,1,0:T(8,128)} async-done(((f32[7,7,1536]{2,1,0:T(8,128)}), f32[7,7,1536]{2,1,0:T(8,128)}) %all-reduce.5.cloned.1.call-update) | async-done | bytes 301072 | tf_op jit(solution)/shard_map/psum | solution.py:102
  889.0 7.1 fusion.72
  896.2 67.4 %all-reduce.7.cloned.1.call-done = f32[7,7,1536]{2,1,0:T(8,128)} async-done(((f32[7,7,1536]{2,1,0:T(8,128)}), f32[7,7,1536]{2,1,0:T(8,128)}) %all-reduce.7.cloned.1.call-update) | async-done | bytes 301072 | tf_op jit(solution)/shard_map/psum | solution.py:101
  963.5 1.7 copy.27
  (254 shorter events, 1.7 us)
Async XLA Ops:
  7.2 110.4 %all-gather.3.cloned.1.call-start = ((), (), s32[]{:S(2)}) async-start(), calls=%async_computation | async-start | bytes 9732096 | tf_op jit(solution)/shard_map/all_gather | solution.py:47
  7.9 212.9 %all-gather.5.cloned.1.call-start = ((), (), s32[]{:S(2)}) async-start(), calls=%async_computation.1 | async-start | bytes 9732096 | tf_op jit(solution)/shard_map/all_gather | solution.py:48
  8.7 880.0 %all-reduce.5.cloned.1.call-start = ((), (), s32[]{:S(2)}) async-start(), calls=%async_computation.2 | async-start | bytes 688128 | tf_op jit(solution)/shard_map/psum | solution.py:102
  10.3 8.0 collective-permute-start
  14.8 6.5 collective-permute-start.1
  21.4 6.7 collective-permute-start.2
  25.8 7.7 collective-permute-start.3
  253.1 6.7 collective-permute-start.4
  257.2 6.5 collective-permute-start.5
  263.9 371.0 %collective-permute-start.6 = (bf16[1,14,3,1536]{3,2,1,0:T(4,128)(2,1)S(1)}, bf16[1,14,3,1536]{3,2,1,0:T(4,128)(2,1)S(1)}, u32[]{:S(2)}, u32[]{:S(2)}) collective-permute-start(bf16[1,14,3,1536]{3,2,1,0:T(4,128)(2,1)S(1)} %get-tuple-element.113), channel_id=1, source_target_pairs={{0,32},{1,33},{2,34},{3,35},{4,36},{5,37},{6,38},{7,39},{8,40},{9,... | collective-permute-start | bytes 387080 | tf_op jit(solution)/shard_map/ppermute | solution.py:17
  268.2 366.7 %collective-permute-start.7 = (bf16[1,14,3,1536]{3,2,1,0:T(4,128)(2,1)S(1)}, bf16[1,14,3,1536]{3,2,1,0:T(4,128)(2,1)S(1)}, u32[]{:S(2)}, u32[]{:S(2)}) collective-permute-start(bf16[1,14,3,1536]{3,2,1,0:T(4,128)(2,1)S(1)} %get-tuple-element.114), channel_id=1, source_target_pairs={{32,0},{33,1},{34,2},{35,3},{36,4},{37,5},{38,6},{39,7},{40,8},{41... | collective-permute-start | bytes 387080 | tf_op jit(solution)/shard_map/ppermute | solution.py:18
  270.3 693.2 %all-reduce.7.cloned.1.call-start = ((), (), s32[]{:S(2)}) async-start(), calls=%async_computation.3 | async-start | bytes 688128 | tf_op jit(solution)/shard_map/psum | solution.py:101
  635.6 253.0 %copy-start.16 = (f32[1536]{0:T(1024)S(1)}, f32[1536]{0:T(1024)}, u32[]{:S(2)}) copy-start(f32[1536]{0:T(1024)} %copy-done.15) | copy-start | bytes 18436
  635.6 253.0 %copy-start.18 = (f32[1536]{0:T(1024)S(1)}, f32[1536]{0:T(1024)}, u32[]{:S(2)}) copy-start(f32[1536]{0:T(1024)} %copy-done.17) | copy-start | bytes 18436
  635.7 253.0 %copy-start.20 = (f32[1536]{0:T(1024)S(1)}, f32[1536]{0:T(1024)}, u32[]{:S(2)}) copy-start(f32[1536]{0:T(1024)} %copy-done.19) | copy-start | bytes 18436
  635.7 253.0 %copy-start.22 = (f32[1536]{0:T(1024)S(1)}, f32[1536]{0:T(1024)}, u32[]{:S(2)}) copy-start(f32[1536]{0:T(1024)} %copy-done.21) | copy-start | bytes 18436
  635.7 253.0 %copy-start.24 = (f32[1536]{0:T(1024)S(1)}, f32[1536]{0:T(1024)}, u32[]{:S(2)}) copy-start(f32[1536]{0:T(1024)} %copy-done.23) | copy-start | bytes 18436
  635.7 253.0 %copy-start.26 = (f32[1536]{0:T(1024)S(1)}, f32[1536]{0:T(1024)}, u32[]{:S(2)}) copy-start(f32[1536]{0:T(1024)} %copy-done.25) | copy-start | bytes 18436
  635.7 253.0 %copy-start.28 = (f32[1536]{0:T(1024)S(1)}, f32[1536]{0:T(1024)}, u32[]{:S(2)}) copy-start(f32[1536]{0:T(1024)} %copy-done.27) | copy-start | bytes 18436
  635.7 253.0 %copy-start.30 = (f32[1536]{0:T(1024)S(1)}, f32[1536]{0:T(1024)}, u32[]{:S(2)}) copy-start(f32[1536]{0:T(1024)} %copy-done.29) | copy-start | bytes 18436
  635.7 253.0 %copy-start.32 = (f32[1536]{0:T(1024)S(1)}, f32[1536]{0:T(1024)}, u32[]{:S(2)}) copy-start(f32[1536]{0:T(1024)} %copy-done.31) | copy-start | bytes 18436
  635.7 253.0 %copy-start.34 = (f32[1536]{0:T(1024)S(1)}, f32[1536]{0:T(1024)}, u32[]{:S(2)}) copy-start(f32[1536]{0:T(1024)} %copy-done.33) | copy-start | bytes 18436
  635.7 253.0 %copy-start.36 = (f32[1536]{0:T(1024)S(1)}, f32[1536]{0:T(1024)}, u32[]{:S(2)}) copy-start(f32[1536]{0:T(1024)} %copy-done.35) | copy-start | bytes 18436
  635.7 253.0 %copy-start.38 = (f32[1536]{0:T(1024)S(1)}, f32[1536]{0:T(1024)}, u32[]{:S(2)}) copy-start(f32[1536]{0:T(1024)} %copy-done.37) | copy-start | bytes 18436
  635.8 253.0 %copy-start.40 = (f32[1536]{0:T(1024)S(1)}, f32[1536]{0:T(1024)}, u32[]{:S(2)}) copy-start(f32[1536]{0:T(1024)} %copy-done.39) | copy-start | bytes 18436
  635.8 253.0 %copy-start.42 = (f32[1536]{0:T(1024)S(1)}, f32[1536]{0:T(1024)}, u32[]{:S(2)}) copy-start(f32[1536]{0:T(1024)} %copy-done.41) | copy-start | bytes 18436
  635.8 253.0 %copy-start.44 = (f32[1536]{0:T(1024)S(1)}, f32[1536]{0:T(1024)}, u32[]{:S(2)}) copy-start(f32[1536]{0:T(1024)} %copy-done.43) | copy-start | bytes 18436
  635.8 253.0 %copy-start.46 = (f32[1536]{0:T(1024)S(1)}, f32[1536]{0:T(1024)}, u32[]{:S(2)}) copy-start(f32[1536]{0:T(1024)} %copy-done.45) | copy-start | bytes 18436
  635.8 253.0 %copy-start.48 = (f32[1536]{0:T(1024)S(1)}, f32[1536]{0:T(1024)}, u32[]{:S(2)}) copy-start(f32[1536]{0:T(1024)} %copy-done.47) | copy-start | bytes 18436
  635.8 253.0 %copy-start.50 = (f32[1536]{0:T(1024)S(1)}, f32[1536]{0:T(1024)}, u32[]{:S(2)}) copy-start(f32[1536]{0:T(1024)} %copy-done.49) | copy-start | bytes 18436
  635.8 253.0 %copy-start.52 = (f32[1536]{0:T(1024)S(1)}, f32[1536]{0:T(1024)}, u32[]{:S(2)}) copy-start(f32[1536]{0:T(1024)} %copy-done.51) | copy-start | bytes 18436
  635.8 253.0 %copy-start.54 = (f32[1536]{0:T(1024)S(1)}, f32[1536]{0:T(1024)}, u32[]{:S(2)}) copy-start(f32[1536]{0:T(1024)} %copy-done.53) | copy-start | bytes 18436
  635.8 253.0 %copy-start.56 = (f32[1536]{0:T(1024)S(1)}, f32[1536]{0:T(1024)}, u32[]{:S(2)}) copy-start(f32[1536]{0:T(1024)} %copy-done.55) | copy-start | bytes 18436
  635.8 253.0 %copy-start.58 = (f32[1536]{0:T(1024)S(1)}, f32[1536]{0:T(1024)}, u32[]{:S(2)}) copy-start(f32[1536]{0:T(1024)} %copy-done.57) | copy-start | bytes 18436
  635.9 253.0 %copy-start.60 = (f32[1536]{0:T(1024)S(1)}, f32[1536]{0:T(1024)}, u32[]{:S(2)}) copy-start(f32[1536]{0:T(1024)} %copy-done.59) | copy-start | bytes 18436
  635.9 253.0 %copy-start.62 = (f32[1536]{0:T(1024)S(1)}, f32[1536]{0:T(1024)}, u32[]{:S(2)}) copy-start(f32[1536]{0:T(1024)} %copy-done.61) | copy-start | bytes 18436
  635.9 253.0 %copy-start.64 = (f32[1536]{0:T(1024)S(1)}, f32[1536]{0:T(1024)}, u32[]{:S(2)}) copy-start(f32[1536]{0:T(1024)} %copy-done.63) | copy-start | bytes 18436
  635.9 253.0 %copy-start.66 = (f32[1536]{0:T(1024)S(1)}, f32[1536]{0:T(1024)}, u32[]{:S(2)}) copy-start(f32[1536]{0:T(1024)} %copy-done.65) | copy-start | bytes 18436
  635.9 253.0 %copy-start.68 = (f32[1536]{0:T(1024)S(1)}, f32[1536]{0:T(1024)}, u32[]{:S(2)}) copy-start(f32[1536]{0:T(1024)} %copy-done.67) | copy-start | bytes 18436
  635.9 253.0 %copy-start.70 = (f32[1536]{0:T(1024)S(1)}, f32[1536]{0:T(1024)}, u32[]{:S(2)}) copy-start(f32[1536]{0:T(1024)} %copy-done.69) | copy-start | bytes 18436
  635.9 253.0 %copy-start.72 = (f32[1536]{0:T(1024)S(1)}, f32[1536]{0:T(1024)}, u32[]{:S(2)}) copy-start(f32[1536]{0:T(1024)} %copy-done.71) | copy-start | bytes 18436
  635.9 253.0 %copy-start.74 = (f32[1536]{0:T(1024)S(1)}, f32[1536]{0:T(1024)}, u32[]{:S(2)}) copy-start(f32[1536]{0:T(1024)} %copy-done.73) | copy-start | bytes 18436
  635.9 253.0 %copy-start.76 = (f32[1536]{0:T(1024)S(1)}, f32[1536]{0:T(1024)}, u32[]{:S(2)}) copy-start(f32[1536]{0:T(1024)} %copy-done.75) | copy-start | bytes 18436
  635.9 253.0 %copy-start.77 = (f32[1536]{0:T(1024)S(1)}, f32[1536]{0:T(1024)}, u32[]{:S(2)}) copy-start(f32[1536]{0:T(1024)} %get-tuple-element.92) | copy-start | bytes 18436
  636.0 253.0 %copy-start.78 = (f32[1536]{0:T(1024)S(1)}, f32[1536]{0:T(1024)}, u32[]{:S(2)}) copy-start(f32[1536]{0:T(1024)} %get-tuple-element.93) | copy-start | bytes 18436
  636.0 253.0 %copy-start.79 = (f32[1536]{0:T(1024)S(1)}, f32[1536]{0:T(1024)}, u32[]{:S(2)}) copy-start(f32[1536]{0:T(1024)} %get-tuple-element.94) | copy-start | bytes 18436
  636.0 253.0 %copy-start.80 = (f32[1536]{0:T(1024)S(1)}, f32[1536]{0:T(1024)}, u32[]{:S(2)}) copy-start(f32[1536]{0:T(1024)} %get-tuple-element.95) | copy-start | bytes 18436
  636.0 253.0 %copy-start.81 = (f32[1536]{0:T(1024)S(1)}, f32[1536]{0:T(1024)}, u32[]{:S(2)}) copy-start(f32[1536]{0:T(1024)} %get-tuple-element.96) | copy-start | bytes 18436
  (52 other events, 1896.2 us)
Sparse Core Ops, SparseCore 0:
  10.6 106.9 all-gather.2
  120.1 100.5 all-gather.4
  270.4 618.1 all-reduce.4
  891.3 72.1 all-reduce.6
